TPU v7x, 32 devices: a whole 2x2x4 slice. The times are simulated.
32 devices in a mesh: wide: 8 (over z, x), blk: 4 (over y, core).
Axes of the slice: x: 2, y: 2, z: 4, core: 2. Of those that a mesh axis runs over, the one named last changes fastest.
Arguments:
- patches: bfloat16 [64, 512, 768], P('wide', 'blk'), may hold values from -6 to 6
- pos_ids: int32 [64, 512], P('wide', 'blk'), may hold values from 0 to 639, as said below
- lengths: int32 [64], P('wide'), may hold values from 64 to 512, as said below
- pos_table: bfloat16 [768, 640], replicated, may hold values from -3 to 3
- ln1_gain: bfloat16 [768], replicated, may hold values from 0.5 to 1.5
- ln1_bias: bfloat16 [768], replicated, may hold values from -3 to 3
- w_qkv: bfloat16 [768, 2304], replicated, may hold values from -0.21875 to 0.21875
- q_bias: bfloat16 [768], replicated, may hold values from -3 to 3
- v_bias: bfloat16 [768], replicated, may hold values from -3 to 3
- w_proj: bfloat16 [768, 768], replicated, may hold values from -2.5 to 2.5
- proj_bias: bfloat16 [768], replicated, may hold values from -3 to 3
- ln2_gain: bfloat16 [768], replicated, may hold values from 0.5 to 1.5
- ln2_bias: bfloat16 [768], replicated, may hold values from -3 to 3
- w_fc1: bfloat16 [768, 3072], replicated, may hold values from -0.21875 to 0.21875
- fc1_bias: bfloat16 [3072], replicated, may hold values from -3 to 3
- w_fc2: bfloat16 [3072, 768], replicated, may hold values from -0.109375 to 0.109375
- fc2_bias: bfloat16 [768], replicated, may hold values from -3 to 3
- cotangent: bfloat16 [64, 512, 768], P('wide', 'blk'), may hold values from -6 to 6
Outputs:
- mixed: bfloat16 [64, 512, 768], P('wide', 'blk')
- patches_grad: bfloat16 [64, 512, 768], P('wide', 'blk')
- pos_table_grad: float32 [768, 640], P(('wide', 'blk'))
- ln1_gain_grad: float32 [768], P(('wide', 'blk'))
- ln1_bias_grad: float32 [768], P(('wide', 'blk'))
- w_qkv_grad: float32 [768, 2304], P(('wide', 'blk'))
- q_bias_grad: float32 [768], P(('wide', 'blk'))
- v_bias_grad: float32 [768], P(('wide', 'blk'))
- w_proj_grad: float32 [768, 768], P(('wide', 'blk'))
- proj_bias_grad: float32 [768], P(('wide', 'blk'))
- ln2_gain_grad: float32 [768], P(('wide', 'blk'))
- ln2_bias_grad: float32 [768], P(('wide', 'blk'))
- w_fc1_grad: float32 [768, 3072], P(('wide', 'blk'))
- fc1_bias_grad: float32 [3072], P(('wide', 'blk'))
- w_fc2_grad: float32 [3072, 768], P(('wide', 'blk'))
- fc2_bias_grad: float32 [768], P(('wide', 'blk'))
Inputs may be any that keep to these rules, and one draw needn't show every extreme that they name: `lengths`: in every aligned block of 8 samples one sample, drawn from the seed, has all 512 slots valid and another exactly 64; slots at or past a sample's length are padding. `pos_ids`: the ids of one sample are distinct.
All inputs are finite; a program needn't handle non-finite values.
Results may differ from a plain program's by a relative error of at most 0.017.
Values may be sent and summed in bfloat16 or wider, within the bound.
No kernel may reach another device: no remote copies, remote signals or barrier semaphores. Data moves between devices by JAX's collectives and lax.ppermute only.
A program may use at most 256 MiB of HBM per device.

v0:
```python
import jax
import jax.numpy as jnp
from jax import lax
from jax.sharding import PartitionSpec as P

HEADS = 12


epsilon = 1e-06
topmost_level = lax.Precision.HIGHEST
masked_score = -1e30


def normalize(stream):
    center = stream - jnp.mean(stream, axis=-1, keepdims=True)
    inverse = lax.rsqrt(jnp.mean(center * center, axis=-1, keepdims=True) + epsilon)
    return (center * inverse, inverse)


def normalize_backward(grad_normed, normed, inverse):
    return inverse * (
        grad_normed
        - jnp.mean(grad_normed, axis=-1, keepdims=True)
        - normed * jnp.mean(grad_normed * normed, axis=-1, keepdims=True)
    )


def product(remaining_part, right):
    return jnp.dot(remaining_part, right, preferred_element_type=jnp.float32)


def product_back(remaining_part, right):
    return lax.dot_general(
        remaining_part, right, (((1,), (1,)), ((), ())), preferred_element_type=jnp.float32
    )


def contract_rows(remaining_part, right):
    return lax.dot_general(
        remaining_part, right, (((0,), (0,)), ((), ())), preferred_element_type=jnp.float32
    )


def score_piece(queries, key_piece, lengths, heads):
    samples_here, rows_here = (key_piece.shape[0], key_piece.shape[1])
    key_heads = key_piece.reshape(samples_here, rows_here, heads, -1)
    scores = jnp.einsum("sqhd,skhd->shqk", queries, key_heads, preferred_element_type=jnp.float32)
    scores = scores * key_heads.shape[-1] ** (-0.5)
    key_place = lax.iota(jnp.int32, rows_here)
    visible = (key_place[None, :] < lengths[:, None])[:, None, None, :]
    return (jnp.where(visible, scores, masked_score), visible, key_heads)


def attend_forward(state_now, pieces, queries, lengths, heads):
    running_max, running_sum, running_out = state_now
    key_piece, value_piece = pieces
    scores, visible, key_heads = score_piece(queries, key_piece, lengths, heads)
    value_heads = value_piece.reshape(key_heads.shape)
    new_max = jnp.maximum(running_max, jnp.max(scores, axis=-1))
    weights = jnp.where(visible, jnp.exp(scores - new_max[..., None]), 0.0)
    running_sum = jnp.sum(weights, axis=-1)
    update = jnp.einsum(
        "shqk,skhd->sqhd",
        weights.astype(jnp.bfloat16),
        value_heads,
        preferred_element_type=jnp.float32,
    )
    running_out = update
    return (new_max, running_sum, running_out)


def attend_backward(pieces, queries, grad_heads, log_total, delta, lengths, heads):
    key_piece, value_piece = pieces
    samples_here, rows_here = (key_piece.shape[0], key_piece.shape[1])
    scores, visible, key_heads = score_piece(queries, key_piece, lengths, heads)
    value_heads = value_piece.reshape(key_heads.shape)
    scale = key_heads.shape[-1] ** (-0.5)
    weights = jnp.where(visible, jnp.exp(scores - log_total[..., None]), 0.0)
    grad_weights = jnp.einsum(
        "sqhd,skhd->shqk", grad_heads, value_heads, preferred_element_type=jnp.float32
    )
    grad_scores = (weights * (grad_weights - delta[..., None])).astype(jnp.bfloat16)
    grad_queries = (
        jnp.einsum("shqk,skhd->sqhd", grad_scores, key_heads, preferred_element_type=jnp.float32)
        * scale
    )
    grad_keys = (
        jnp.einsum("shqk,sqhd->skhd", grad_scores, queries, preferred_element_type=jnp.float32)
        * scale
    )
    grad_values = jnp.einsum(
        "shqk,sqhd->skhd",
        weights.astype(jnp.bfloat16),
        grad_heads,
        preferred_element_type=jnp.float32,
    )
    key_grads = jnp.concatenate(
        [
            grad_keys.reshape(samples_here, rows_here, -1),
            grad_values.reshape(samples_here, rows_here, -1),
        ],
        axis=-1,
    )
    return (grad_queries, key_grads)


def shards(
    patches,
    pos_ids,
    lengths,
    pos_table,
    ln1_gain,
    ln1_bias,
    w_qkv,
    q_bias,
    v_bias,
    w_proj,
    proj_bias,
    ln2_gain,
    ln2_bias,
    w_fc1,
    fc1_bias,
    w_fc2,
    fc2_bias,
    cotangent,
):
    samples_here, rows_here, width = patches.shape
    heads = HEADS
    head_dim = width // heads
    tokens_here = samples_here * rows_here
    positions = pos_table.shape[1]
    gain_one = ln1_gain.astype(jnp.float32)
    gain_two = ln2_gain.astype(jnp.float32)
    onehot = (pos_ids.reshape(tokens_here, 1) == lax.iota(jnp.int32, positions)[None, :]).astype(
        jnp.float32
    )
    embedded = lax.dot_general(
        onehot.astype(jnp.bfloat16),
        pos_table,
        (((1,), (1,)), ((), ())),
        preferred_element_type=jnp.float32,
    )
    stream = patches.reshape(tokens_here, width).astype(jnp.float32) + embedded
    normed_one, inverse_one = normalize(stream)
    attn_in = (normed_one * gain_one + ln1_bias.astype(jnp.float32)).astype(jnp.bfloat16)
    bias_row = jnp.concatenate([q_bias, jnp.zeros_like(q_bias), v_bias]).astype(jnp.float32)
    joined = (product(attn_in, w_qkv) + bias_row).astype(jnp.bfloat16)
    queries = joined[:, :width].reshape(samples_here, rows_here, heads, head_dim)
    key_rows = joined[:, width : 2 * width].reshape(samples_here, rows_here, width)
    value_rows = joined[:, 2 * width :].reshape(samples_here, rows_here, width)
    initial_state = (
        jnp.full((samples_here, heads, rows_here), masked_score, jnp.float32),
        jnp.zeros((samples_here, heads, rows_here), jnp.float32),
        jnp.zeros((samples_here, rows_here, heads, head_dim), jnp.float32),
    )
    running_max, running_sum, running_out = attend_forward(
        initial_state,
        (
            lax.all_gather(key_rows, "blk", axis=1, tiled=True),
            lax.all_gather(value_rows, "blk", axis=1, tiled=True),
        ),
        queries,
        lengths,
        heads,
    )
    attended = running_out / jnp.transpose(running_sum, (0, 2, 1))[..., None]
    log_total = running_max + jnp.log(running_sum)
    attn_low = attended.reshape(tokens_here, width).astype(jnp.bfloat16)
    stream_mid = stream + product(attn_low, w_proj) + proj_bias.astype(jnp.float32)
    normed_two, inverse_two = normalize(stream_mid)
    mlp_in = (normed_two * gain_two + ln2_bias.astype(jnp.float32)).astype(jnp.bfloat16)
    pre_act = product(mlp_in, w_fc1) + fc1_bias.astype(jnp.float32)
    activated, gelu_back = jax.vjp(
        lambda pre_value: jax.nn.gelu(pre_value, approximate=False), pre_act
    )
    act_low = activated.astype(jnp.bfloat16)
    result = stream_mid + product(act_low, w_fc2) + fc2_bias.astype(jnp.float32)
    mixed = result.astype(jnp.bfloat16).reshape(samples_here, rows_here, width)
    grad_two = cotangent.reshape(tokens_here, width)
    grad_out = grad_two.astype(jnp.float32)
    fc2_bias_grad = jnp.sum(grad_out, axis=0)
    w_fc2_grad = contract_rows(act_low, grad_two)
    (grad_pre,) = gelu_back(product_back(grad_two, w_fc2))
    grad_pre_low = grad_pre.astype(jnp.bfloat16)
    fc1_bias_grad = jnp.sum(grad_pre_low.astype(jnp.float32), axis=0)
    w_fc1_grad = contract_rows(mlp_in, grad_pre_low)
    grad_mlp_in = product_back(grad_pre_low, w_fc1)
    ln2_gain_grad = jnp.sum(grad_mlp_in * normed_two, axis=0)
    ln2_bias_grad = jnp.sum(grad_mlp_in, axis=0)
    grad_mid = grad_out + normalize_backward(grad_mlp_in * gain_two, normed_two, inverse_two)
    grad_one = grad_mid.astype(jnp.bfloat16)
    proj_bias_grad = jnp.sum(grad_one.astype(jnp.float32), axis=0)
    w_proj_grad = contract_rows(attn_low, grad_one)
    grad_attended = product_back(grad_one, w_proj).astype(jnp.bfloat16)
    grad_attended = grad_attended.reshape(samples_here, rows_here, heads, head_dim)
    delta = jnp.einsum("sqhd,sqhd->shq", grad_attended.astype(jnp.float32), attended)
    back_result = attend_backward(
        (
            lax.all_gather(key_rows, "blk", axis=1, tiled=True),
            lax.all_gather(value_rows, "blk", axis=1, tiled=True),
        ),
        queries,
        grad_attended,
        log_total,
        delta,
        lengths,
        heads,
    )
    grad_queries = back_result[0]
    own_pairs = lax.psum_scatter(
        back_result[1].astype(jnp.bfloat16), "blk", scatter_dimension=1, tiled=True
    ).astype(jnp.float32)
    grad_joined = jnp.concatenate(
        [grad_queries.reshape(tokens_here, width), own_pairs.reshape(tokens_here, 2 * width)],
        axis=1,
    ).astype(jnp.bfloat16)
    joined_sums = jnp.sum(grad_joined.astype(jnp.float32), axis=0)
    q_bias_grad = joined_sums[:width]
    v_bias_grad = joined_sums[2 * width :]
    w_qkv_grad = contract_rows(attn_in, grad_joined)
    grad_attn_in = product_back(grad_joined, w_qkv)
    ln1_gain_grad = jnp.sum(grad_attn_in * normed_one, axis=0)
    ln1_bias_grad = jnp.sum(grad_attn_in, axis=0)
    grad_stream = grad_mid + normalize_backward(grad_attn_in * gain_one, normed_one, inverse_one)
    patches_grad = grad_stream.astype(jnp.bfloat16).reshape(samples_here, rows_here, width)
    pos_table_grad = lax.dot_general(
        grad_stream,
        onehot,
        (((0,), (0,)), ((), ())),
        precision=topmost_level,
        preferred_element_type=jnp.float32,
    )
    gradients = [
        pos_table_grad,
        ln1_gain_grad,
        ln1_bias_grad,
        w_qkv_grad,
        q_bias_grad,
        v_bias_grad,
        w_proj_grad,
        proj_bias_grad,
        ln2_gain_grad,
        ln2_bias_grad,
        w_fc1_grad,
        fc1_bias_grad,
        w_fc2_grad,
        fc2_bias_grad,
    ]
    shares = (
        lax.psum_scatter(gradients[0], ("wide", "blk"), scatter_dimension=0, tiled=True),
        lax.psum_scatter(gradients[1], ("wide", "blk"), scatter_dimension=0, tiled=True),
        lax.psum_scatter(gradients[2], ("wide", "blk"), scatter_dimension=0, tiled=True),
        lax.psum_scatter(gradients[3], ("wide", "blk"), scatter_dimension=0, tiled=True),
        lax.psum_scatter(gradients[4], ("wide", "blk"), scatter_dimension=0, tiled=True),
        lax.psum_scatter(gradients[5], ("wide", "blk"), scatter_dimension=0, tiled=True),
        lax.psum_scatter(gradients[6], ("wide", "blk"), scatter_dimension=0, tiled=True),
        lax.psum_scatter(gradients[7], ("wide", "blk"), scatter_dimension=0, tiled=True),
        lax.psum_scatter(gradients[8], ("wide", "blk"), scatter_dimension=0, tiled=True),
        lax.psum_scatter(gradients[9], ("wide", "blk"), scatter_dimension=0, tiled=True),
        lax.psum_scatter(gradients[10], ("wide", "blk"), scatter_dimension=0, tiled=True),
        lax.psum_scatter(gradients[11], ("wide", "blk"), scatter_dimension=0, tiled=True),
        lax.psum_scatter(gradients[12], ("wide", "blk"), scatter_dimension=0, tiled=True),
        lax.psum_scatter(gradients[13], ("wide", "blk"), scatter_dimension=0, tiled=True),
    )
    return (
        mixed,
        patches_grad,
        shares[0],
        shares[1],
        shares[2],
        shares[3],
        shares[4],
        shares[5],
        shares[6],
        shares[7],
        shares[8],
        shares[9],
        shares[10],
        shares[11],
        shares[12],
        shares[13],
    )


def solution(mesh):
    in_specs = (
        P("wide", "blk", None),
        P("wide", "blk"),
        P("wide"),
        P(),
        P(),
        P(),
        P(),
        P(),
        P(),
        P(),
        P(),
        P(),
        P(),
        P(),
        P(),
        P(),
        P(),
        P("wide", "blk", None),
    )
    out_specs = (
        P("wide", "blk", None),
        P("wide", "blk", None),
        P(("wide", "blk"), None),
        P(("wide", "blk")),
        P(("wide", "blk")),
        P(("wide", "blk"), None),
        P(("wide", "blk")),
        P(("wide", "blk")),
        P(("wide", "blk"), None),
        P(("wide", "blk")),
        P(("wide", "blk")),
        P(("wide", "blk")),
        P(("wide", "blk"), None),
        P(("wide", "blk")),
        P(("wide", "blk"), None),
        P(("wide", "blk")),
    )
    return jax.shard_map(shards, mesh=mesh, in_specs=in_specs, out_specs=out_specs, check_vma=False)
```

profile of v0, /device:TPU:0, one launch (start us, length us, event | category | flops | bytes accessed | tf_op | source)
XLA Modules:
  0.0 1022.3 jit_solution(2052366673927181097)
XLA Ops:
  30.4 38.6 %all-gather.5.cloned.1.call-done = bf16[8,512,768]{2,1,0:T(8,128)(2,1)} async-done(((bf16[8,128,768]{2,1,0:T(8,128)(2,1)}), bf16[8,512,768]{2,1,0:T(8,128)(2,1)}) %all-gather.5.cloned.1.call-update) | async-done | bytes 6291472 | tf_op jit(solution)/shard_map/all_gather | solution.py:159
  77.7 17.4 %fusion.3 = (f32[8,12,128]{2,1,0:T(8,128)S(1)}, f32[8,12,128,512]{3,2,1,0:T(8,128)}) fusion(pred[8,512]{1,0:T(8,128)(4,1)S(1)} %iota_compare_fusion.2, bf16[8,512,12,64]{1,3,2,0:T(8,128)(2,1)} %bitcast.78, bf16[8,128,12,64]{1,0,3,2:T(8,128)(2,1)} %bitcast.81), kind=kOutput, calls=%fused_computation.8 | convolution fusion | flops 824168448 | bytes 33083392 | tf_op jit(solution)/shard_map/sqhd,skhd->shqk/dot_general | solution.py:47
  95.1 11.9 %fusion = f32[8,12,128]{2,1,0:T(8,128)S(1)} fusion(f32[8,12,128,512]{3,2,1,0:T(8,128)} %get-tuple-element.47, f32[8,12,128]{2,1,0:T(8,128)S(1)} %broadcast_maximum_fusion, pred[8,512]{1,0:T(8,128)(4,1)S(1)} %iota_compare_fusion.2), kind=kLoop, calls=%fused_computation.4 | loop fusion | flops 31444992 | bytes 25268224 | tf_op jit(solution)/shard_map/reduce_sum | solution.py:61
  108.3 8.8 all-gather.3.cloned.1.call-done
  125.7 15.8 %fusion.58 = (bf16[8,128,12,64]{1,3,2,0:T(8,128)(2,1)}, f32[8,128,12,64]{1,3,2,0:T(8,128)}) fusion(f32[8,128,12]{1,2,0:T(8,128)} %bitcast.103, bf16[8,512,12,64]{1,3,2,0:T(8,128)(2,1)} %bitcast.83, f32[8,12,128,512]{3,2,1,0:T(8,128)} %get-tuple-element.47, f32[8,12,128]{2,1,0:T(8,128)} %copy-done.14, pred[8,512]{1,0:T(8,128)(4,1)S(1)} %iota_compare_fusion.2), kind=kOutput, calls=%fused_computation.111 | convolution fusion | flops 838336512 | bytes 36278272 | tf_op jit(solution)/shard_map/shqk,skhd->sqhd/dot_general | solution.py:62
  149.5 35.2 %multiply_convert_fusion.2 = (bf16[1024,3072]{1,0:T(8,128)(2,1)}, f32[1024,3072]{1,0:T(8,128)}, f32[1024,3072]{1,0:T(8,128)}) fusion(f32[3072]{0:T(1024)S(1)} %copy-done.25, bf16[768,3072]{1,0:T(8,128)(2,1)S(1)} %bitcast.105, f32[1024,768]{1,0:T(8,128)S(1)} %get-tuple-element.51, f32[768]{0:T(1024)S(1)} %copy-done.15, f32[768]{0:T(1024)S(1)} %convert_element_type.114, ...), kind=kOutput, calls=%fused_computation.16 | convolution fusion | flops 5043388416 | bytes 39348224 | tf_op jit(solution)/shard_map/dot_general | solution.py:29
  184.7 18.8 %convert_reduce_fusion = (f32[3072]{0:T(1024)}, bf16[1024,3072]{1,0:T(8,128)(2,1)}) fusion(f32[1024,3072]{1,0:T(8,128)} %get-tuple-element.38, bf16[1024,768]{1,0:T(8,128)(2,1)} %bitcast.86, bf16[3072,768]{1,0:T(8,128)(2,1)} %param.33, f32[1024,3072]{1,0:T(8,128)} %get-tuple-element.52, f32[3072]{0:T(1024)S(1)} %copy-done.25), kind=kOutput, calls=%fused_computation.12 | convolution fusion | flops 4885312512 | bytes 37773312 | tf_op jit(solution)/shard_map/dot_general | solution.py:33
  203.5 10.1 multiply_reduce_fusion.1
  225.9 13.3 %fusion.20 = bf16[8,12,64,512]{3,2,1,0:T(8,128)(2,1)} fusion(f32[8,12,128,512]{3,2,1,0:T(8,128)} %get-tuple-element.47, f32[8,12,128]{2,1,0:T(8,128)} %log_add_fusion, pred[8,512]{1,0:T(8,128)(4,1)S(1)} %iota_compare_fusion.2, bf16[8,128,12,64]{1,0,3,2:T(8,128)(2,1)} %bitcast.95), kind=kOutput, calls=%fused_computation.39 | convolution fusion | flops 839909376 | bytes 33083392 | tf_op jit(solution)/shard_map/shqk,sqhd->skhd/dot_general | solution.py:91
  242.3 19.9 %multiply_convert_fusion = bf16[8,12,128,512]{3,2,1,0:T(8,128)(2,1)} fusion(f32[8,12,128,512]{3,2,1,0:T(8,128)} %get-tuple-element.47, f32[8,12,128]{2,1,0:T(8,128)S(1)} %multiply_reduce_fusion, f32[8,12,128]{2,1,0:T(8,128)S(1)} %copy-done.17, pred[8,512]{1,0:T(8,128)(4,1)S(1)} %iota_compare_fusion.2, bf16[8,512,12,64]{1,3,2,0:T(8,128)(2,1)} %bitcast.84, ...), kind=kOutput, calls=%fused_computation | convolution fusion | flops 849346560 | bytes 45715456 | tf_op jit(solution)/shard_map/sqhd,skhd->shqk/dot_general | solution.py:79
  262.1 9.0 multiply_convert_fusion.1
  288.5 10.5 %pad_maximum_fusion = bf16[8,512,1536]{2,1,0:T(8,128)(2,1)} fusion(bf16[8,512,768]{2,1,0:T(8,128)(2,1)} %copy.64, bf16[8,512,768]{2,1,0:T(8,128)(2,1)} %copy.63), kind=kLoop, calls=%fused_computation.11 | loop fusion | flops 25165824 | bytes 25165824 | tf_op jit(solution)/shard_map/concatenate | solution.py:97
  304.3 11.0 %fusion.60 = f32[3072,768]{1,0:T(8,128)} fusion(bf16[1024,3072]{1,0:T(8,128)(2,1)} %get-tuple-element.37, bf16[1024,768]{1,0:T(8,128)(2,1)} %bitcast.87), kind=kOutput, calls=%fused_computation.113 | convolution fusion | flops 4831838208 | bytes 17301504 | tf_op jit(solution)/shard_map/dot_general | solution.py:39
  316.0 11.9 %fusion.51 = f32[768,3072]{1,0:T(8,128)} fusion(bf16[1024,3072]{1,0:T(8,128)(2,1)} %get-tuple-element.56, f32[1024,768]{1,0:T(8,128)} %copy-done.1, f32[768]{0:T(1024)S(1)} %copy-done.16, f32[768]{0:T(1024)S(1)} %convert_element_type.114, f32[1024]{0:T(1024)S(1)} %add_rsqrt_fusion, f32[1024]{0:T(1024)S(1)} %broadcast_multiply_fusion.4), kind=kOutput, calls=%fused_computation.105 | convolution fusion | flops 4835770368 | bytes 18888704 | tf_op jit(solution)/shard_map/dot_general | solution.py:39
  328.3 11.9 %fusion.29 = bf16[8,128,12,64]{1,3,2,0:T(8,128)(2,1)} fusion(bf16[8,512,12,64]{1,3,2,0:T(8,128)(2,1)} %bitcast.79, bf16[8,12,128,512]{3,2,1,0:T(8,128)(2,1)} %multiply_convert_fusion), kind=kOutput, calls=%fused_computation.71 | convolution fusion | flops 806879232 | bytes 20447232 | tf_op jit(solution)/shard_map/shqk,skhd->sqhd/dot_general | solution.py:84
  347.2 51.1 %reduce-scatter.9.cloned.1.call-done = bf16[8,128,1536]{2,1,0:T(8,128)(2,1)} async-done(((bf16[8,512,1536]{2,1,0:T(8,128)(2,1)}), bf16[8,128,1536]{2,1,0:T(8,128)(2,1)}) %reduce-scatter.9.cloned.1.call-update) | async-done | bytes 3145744 | tf_op jit(solution)/shard_map/reduce_scatter | solution.py:210
  415.1 10.5 %fusion.37 = f32[768,2304]{1,0:T(8,128)} fusion(bf16[1024,1536]{1,0:T(8,128)(2,1)} %bitcast.98, bf16[1024,768]{1,0:T(8,128)(2,1)} %copy.65, f32[1024,768]{1,0:T(8,128)} %copy-done.3, f32[768]{0:T(1024)S(1)} %copy-done.28, f32[768]{0:T(1024)S(1)} %copy-done.21, f32[1024]{0:T(1024)S(1)} %copy-done.23, f32[1024]{0:T(1024)S(1)} %copy-done.19), kind=kOutput, calls=%fused_computation.79 | convolution fusion | flops 3637248000 | bytes 14956544 | tf_op jit(solution)/shard_map/dot_general | solution.py:39
  428.0 10.1 add_convert_fusion.2
  438.9 41.4 %all-reduce.10 = (f32[768]{0:T(1024)}, f32[768]{0:T(1024)}, f32[768]{0:T(1024)}, f32[768]{0:T(1024)}, f32[768]{0:T(1024)}, /*index=5*/f32[768]{0:T(1024)}, f32[768]{0:T(1024)}, f32[3072]{0:T(1024)}, f32[768]{0:T(1024)}) all-reduce(f32[768]{0:T(1024)} %get-tuple-element.18, ...), channel_id=4, replica_groups=mesh['wide'=8,'blk'=4] {'wide','blk'}, use_global_device_ids=true, to_apply=%region_13.14.clone | all-reduce | flops 9216 | bytes 73728
  491.6 11.5 %reduce-scatter.13.cloned.1.call-done = f32[24,768]{1,0:T(8,128)} async-done(((f32[768,768]{1,0:T(8,128)}), f32[24,768]{1,0:T(8,128)}) %reduce-scatter.13.cloned.1.call-update) | async-done | bytes 73744 | tf_op jit(solution)/shard_map/reduce_scatter | solution.py:256
  503.2 142.0 %reduce-scatter.17.cloned.1.call-done = f32[96,768]{1,0:T(8,128)} async-done(((f32[3072,768]{1,0:T(8,128)}), f32[96,768]{1,0:T(8,128)}) %reduce-scatter.17.cloned.1.call-update) | async-done | bytes 294928 | tf_op jit(solution)/shard_map/reduce_scatter | solution.py:262
  645.2 140.9 %reduce-scatter.15.cloned.1.call-done = f32[24,3072]{1,0:T(8,128)} async-done(((f32[768,3072]{1,0:T(8,128)}), f32[24,3072]{1,0:T(8,128)}) %reduce-scatter.15.cloned.1.call-update) | async-done | bytes 294928 | tf_op jit(solution)/shard_map/reduce_scatter | solution.py:260
  786.1 103.6 %reduce-scatter.19.cloned.1.call-done = f32[24,640]{1,0:T(8,128)} async-done(((f32[768,640]{1,0:T(8,128)}), f32[24,640]{1,0:T(8,128)}) %reduce-scatter.19.cloned.1.call-update) | async-done | bytes 61456
  889.7 125.5 %reduce-scatter.11.cloned.1.call-done = f32[24,2304]{1,0:T(8,128)} async-done(((f32[768,2304]{1,0:T(8,128)}), f32[24,2304]{1,0:T(8,128)}) %reduce-scatter.11.cloned.1.call-update) | async-done | bytes 221200 | tf_op jit(solution)/shard_map/reduce_scatter | solution.py:253
  (150 shorter events, 126.5 us)
Async XLA Ops:
  7.2 5.8 copy-start
  7.2 61.8 %all-gather.5.cloned.1.call-start = ((), (), s32[]{:S(2)}) async-start(), calls=%async_computation.7 | async-start | bytes 7864320 | tf_op jit(solution)/shard_map/all_gather | solution.py:159
  17.5 6.0 copy-start.26
  19.8 97.2 %all-gather.3.cloned.1.call-start = ((), (), s32[]{:S(2)}) async-start(), calls=%async_computation.6 | async-start | bytes 7864320 | tf_op jit(solution)/shard_map/all_gather | solution.py:160
  20.5 377.7 %reduce-scatter.9.cloned.1.call-start = ((), (), s32[]{:S(2)}) async-start(), calls=%async_computation.8 | async-start | bytes 15728640 | tf_op jit(solution)/shard_map/reduce_scatter | solution.py:210
  95.1 11.9 %copy-start.14 = (f32[8,12,128]{2,1,0:T(8,128)}, f32[8,12,128]{2,1,0:T(8,128)S(1)}, u32[]{:S(2)}) copy-start(f32[8,12,128]{2,1,0:T(8,128)S(1)} %broadcast_maximum_fusion) | copy-start | bytes 147460
  125.7 18.6 %copy-start.29 = (f32[768]{0:T(1024)S(1)}, f32[768]{0:T(1024)}, u32[]{:S(2)}) copy-start(f32[768]{0:T(1024)} %convert_element_type.113) | copy-start | bytes 9220
  141.5 7.9 slice-start
  148.9 64.8 %copy-start.1 = (f32[1024,768]{1,0:T(8,128)}, f32[1024,768]{1,0:T(8,128)S(1)}, u32[]{:S(2)}) copy-start(f32[1024,768]{1,0:T(8,128)S(1)} %get-tuple-element.51) | copy-start | bytes 9437188
  203.5 10.2 copy-start.7
  242.2 19.9 %copy-start.2 = (bf16[96,8,8,128]{3,2,1,0:T(8,128)(2,1)S(1)}, bf16[96,8,8,128]{3,2,1,0:T(8,128)(2,1)}, u32[]{:S(2)}) copy-start(bf16[96,8,8,128]{3,2,1,0:T(8,128)(2,1)} %copy.72) | copy-start | bytes 4718596
  299.1 204.1 %reduce-scatter.13.cloned.1.call-start = ((), (), s32[]{:S(2)}) async-start(), calls=%async_computation.10 | async-start | bytes 2433024 | tf_op jit(solution)/shard_map/reduce_scatter | solution.py:256
  304.3 340.9 %reduce-scatter.17.cloned.1.call-start = ((), (), s32[]{:S(2)}) async-start(), calls=%async_computation.12 | async-start | bytes 9732096 | tf_op jit(solution)/shard_map/reduce_scatter | solution.py:262
  315.4 470.7 %reduce-scatter.15.cloned.1.call-start = ((), (), s32[]{:S(2)}) async-start(), calls=%async_computation.11 | async-start | bytes 9732096 | tf_op jit(solution)/shard_map/reduce_scatter | solution.py:260
  327.9 561.8 %reduce-scatter.19.cloned.1.call-start = ((), (), s32[]{:S(2)}) async-start(), calls=%async_computation.13 | async-start | bytes 2027520
  340.3 58.0 %copy-start.19 = (f32[1024]{0:T(1024)S(1)}, f32[1024]{0:T(1024)}, u32[]{:S(2)}) copy-start(f32[1024]{0:T(1024)} %copy-done.18) | copy-start | bytes 12292
  340.3 58.0 %copy-start.21 = (f32[768]{0:T(1024)S(1)}, f32[768]{0:T(1024)}, u32[]{:S(2)}) copy-start(f32[768]{0:T(1024)} %copy-done.20) | copy-start | bytes 9220
  340.3 58.0 %copy-start.23 = (f32[1024]{0:T(1024)S(1)}, f32[1024]{0:T(1024)}, u32[]{:S(2)}) copy-start(f32[1024]{0:T(1024)} %copy-done.22) | copy-start | bytes 12292
  398.3 8.4 copy-start.4
  398.3 8.4 copy-start.6
  408.8 6.3 copy-start.28
  414.9 600.4 %reduce-scatter.11.cloned.1.call-start = ((), (), s32[]{:S(2)}) async-start(), calls=%async_computation.9 | async-start | bytes 7299072 | tf_op jit(solution)/shard_map/reduce_scatter | solution.py:253
  428.0 10.2 copy-start.8
  428.0 10.2 copy-start.11
  (22 other events, 72.2 us)
Sparse Core Ops, SparseCore 0:
  19.9 49.0 all-gather.4
  70.6 46.3 all-gather.2
  299.2 99.0 reduce-scatter.8
  404.0 99.1 reduce-scatter.12
  510.5 134.6 reduce-scatter.16
  651.5 134.5 reduce-scatter.14
  792.8 96.9 reduce-scatter.18
  896.9 118.2 reduce-scatter.10
where the time goes:
time: 1030 us; the launch traced here: 1020 us
  waiting for transfers between devices  623 us (60%)
  matrix products  229 us (22%)
  local copies, waits for them, and re-layouts  72.9 us (7%)
  blocking collectives  41.4 us (4%)
  other arithmetic  39.6 us (4%)
  between operations  14.9 us (1%)
    reduce_scatter x1, waiting for transfers between devices, shards(): lax.psum_scatter(gradients[12], ('wide', 'blk'), scatter_dimension=0, til...  142 us
    reduce_scatter x1, waiting for transfers between devices, shards(): lax.psum_scatter(gradients[10], ('wide', 'blk'), scatter_dimension=0, til...  141 us
    reduce_scatter x1, waiting for transfers between devices, shards(): lax.psum_scatter(gradients[3], ('wide', 'blk'), scatter_dimension=0, tile...  125 us
    unnamed x9, waiting for transfers between devices  104 us
    dot_general x4, matrix products, product(): return jnp.dot(remaining_part, right, preferred_element_type=jnp.float32)  54.4 us
    reduce_scatter x1, waiting for transfers between devices, shards(): lax.psum_scatter(back_result[1].astype(jnp.bfloat16), 'blk', scatter_dime...  51.1 us
    unnamed x1, blocking collectives  41.4 us
    dot_general x4, matrix products, product_back(): lax.dot_general(remaining_part, right, (((1,), (1,)), ((), ())), preferre...  39.9 us
  transfers between devices with their start and end apart: 8, of which 8 were waited for; matrix products, arithmetic and copies ran while one was open for 14% of the time, Pallas kernels for 0%

commit v1 on v0

v1 whole, which is shorter than its diff:
```python
import functools

import jax
import jax.numpy as jnp
from jax import lax
from jax.experimental import pallas as pl
from jax.experimental.pallas import tpu as pltpu
from jax.sharding import PartitionSpec as P

HEADS = 12
F32, BF16 = jnp.float32, jnp.bfloat16
NN = (((1,), (0,)), ((), ()))
NT = (((1,), (1,)), ((), ()))
TN = (((0,), (0,)), ((), ()))
EPS = 1e-6
MASKED = -1e30
AXES = ("wide", "blk")
MIB = 2**20


def dot(a, b, dims=NN):
    return lax.dot_general(a, b, dims, preferred_element_type=F32)


def whole(shape):
    return pl.BlockSpec(shape, lambda *_: (0,) * len(shape))


def normalize(x):
    center = x - jnp.mean(x, axis=-1, keepdims=True)
    inverse = lax.rsqrt(jnp.mean(center * center, axis=-1, keepdims=True) + EPS)
    return center * inverse, inverse


def normalize_back(g, normed, inverse):
    return inverse * (
        g - jnp.mean(g, axis=-1, keepdims=True) - normed * jnp.mean(g * normed, axis=-1, keepdims=True)
    )


def gelu_both(x):
    cdf = 0.5 + 0.5 * lax.erf(x * 0.7071067811865476)
    return x * cdf, cdf + x * (jnp.exp(x * x * -0.5) * 0.3989422804014327)


def row_sum(x):
    return jnp.sum(x.astype(F32), axis=0, keepdims=True)


def owner_dims(owner, order):
    x, y = (owner // 4) % 2, (owner // 2) % 2
    return (owner % 2,) + ((x, y) if order == "xy" else (y, x)) + (owner // 8,)


def store_packed(ref, order, result, first_row, tile_at):
    per = 24
    for k in range(result.shape[0] // per):
        where = owner_dims(first_row // per + k, order)
        rows = result[k * per : (k + 1) * per]
        for c in range(result.shape[1] // 256):
            two = jnp.concatenate([rows[:, c * 256 : c * 256 + 128], rows[:, c * 256 + 128 : c * 256 + 256]], 0)
            start = (tile_at + 2 * c) * per
            ref[where + (slice(start, start + 2 * per), slice(None))] = two.astype(BF16)


def attend_kernel(
    length_ref, x_ref, ids_ref, table_ref, gain_ref, bias_ref, wqkv_ref, bqkv_ref, wproj_ref, bproj_ref, *rest
):
    stream_ref, joined_ref, probs_ref, low_ref, mid_ref, stream, joined, low = rest[-8:]
    j = pl.program_id(0)
    rows, width = stream.shape
    half = 64

    @pl.when(j == 0)
    def _():
        positions = table_ref.shape[1]
        onehot = (ids_ref[0] == lax.broadcasted_iota(jnp.int32, (rows, positions), 1)).astype(F32).astype(BF16)
        value = x_ref[...].reshape(rows, width).astype(F32) + dot(onehot, table_ref[...], NT)
        stream[...] = value
        stream_ref[0] = value
        normed, _ = normalize(value)
        attn_in = (normed * gain_ref[...].astype(F32) + bias_ref[...].astype(F32)).astype(BF16)
        for c in range(3):
            cols = slice(c * width, (c + 1) * width)
            part = (dot(attn_in, wqkv_ref[:, cols]) + bqkv_ref[:, cols].astype(F32)).astype(BF16)
            if c == 0:
                part = part * jnp.asarray(half**-0.5, BF16)
            joined[:, cols] = part
            joined_ref[0, :, cols] = part

    at = pl.multiple_of(j * 128, 128)
    q = joined[:, pl.ds(at, 128)]
    k = joined[:, pl.ds(pl.multiple_of(width + j * 128, 128), 128)]
    v = joined[:, pl.ds(pl.multiple_of(2 * width + j * 128, 128), 128)]
    v_t = v.T
    lane = lax.broadcasted_iota(jnp.int32, (rows, 128), 1)
    visible = lax.broadcasted_iota(jnp.int32, (rows, rows), 0) < length_ref[0]
    outs = []
    for h in range(2):
        q_h = jnp.where((lane < half) == (h == 0), q, jnp.zeros_like(q))
        scores = jnp.where(visible, dot(k, q_h, NT), MASKED)
        weights = jnp.exp(scores - jnp.max(scores, axis=0, keepdims=True))
        probs = (weights * (1.0 / jnp.sum(weights, axis=0, keepdims=True))).astype(BF16)
        probs_ref[0, h] = probs
        outs.append(dot(v_t[h * half : (h + 1) * half], probs))
    low[:, pl.ds(at, 128)] = jnp.concatenate(outs, 0).T.astype(BF16)

    @pl.when(j == pl.num_programs(0) - 1)
    def _():
        low_ref[0] = low[...]
        mid_ref[0] = stream[...] + dot(low[...], wproj_ref[...]) + bproj_ref[...].astype(F32)


def attend(sample, samples, length, x, ids, table, gain, bias, w_qkv, b_qkv, w_proj, b_proj, previous):
    parts, _, piece, width = x.shape
    rows = parts * piece
    pairs = HEADS // 2
    place = lambda j: (sample, 0, 0)
    ops = [length, x, ids, table, gain, bias, w_qkv, b_qkv, w_proj, b_proj]
    in_specs = [
        pl.BlockSpec(memory_space=pltpu.SMEM),
        pl.BlockSpec((parts, 1, piece, width), lambda j: (0, 0, 0, 0)),
        pl.BlockSpec((1, rows, 1), place),
    ] + [whole(a.shape) for a in ops[3:]]
    shapes = [
        ((samples, rows, width), F32),
        ((samples, rows, 3 * width), BF16),
        ((samples, HEADS, rows, rows), BF16),
        ((samples, rows, width), BF16),
        ((samples, rows, width), F32),
    ]
    aliases = {}
    if previous is not None:
        aliases = {len(ops) + i: i for i in range(len(shapes))}
        ops += list(previous)
        in_specs += [pl.BlockSpec(memory_space=pl.ANY)] * len(shapes)
    return pl.pallas_call(
        attend_kernel,
        grid=(pairs,),
        in_specs=in_specs,
        out_specs=[
            pl.BlockSpec((1, rows, width), place),
            pl.BlockSpec((1, rows, 3 * width), place),
            pl.BlockSpec((1, 2, rows, rows), lambda j: (sample, j, 0, 0)),
            pl.BlockSpec((1, rows, width), place),
            pl.BlockSpec((1, rows, width), place),
        ],
        out_shape=[jax.ShapeDtypeStruct(*s) for s in shapes],
        scratch_shapes=[
            pltpu.VMEM((rows, width), F32),
            pltpu.VMEM((rows, 3 * width), BF16),
            pltpu.VMEM((rows, width), BF16),
        ],
        input_output_aliases=aliases,
        compiler_params=pltpu.CompilerParams(vmem_limit_bytes=56 * MIB),
        cost_estimate=pl.CostEstimate(flops=12 * 10**9, bytes_accessed=30 * 10**6, transcendentals=0),
        name=f"attend_{sample}",
    )(*ops)


def mlp_kernel(
    packed, x_ref, gt_ref, w1_ref, b1_ref, w2_ref, b2_ref, gain_ref, bias_ref,
    mixed_ref, gmid_ref, gone_ref, dw1_ref, dw2_ref, db1_ref, small_ref,
    mlp_in, mlp_in_t, gt, act, gpre, acc, gacc,
):
    j = pl.program_id(0)
    samples, rows, width = x_ref.shape
    piece = gt_ref.shape[2]
    columns = w1_ref.shape[1]
    tile = 2 * piece
    per_sample = rows // tile
    tiles = samples * per_sample

    @pl.when(j == 0)
    def _():
        for i in range(tiles):
            s, t = i // per_sample, i % per_sample
            here = slice(i * tile, (i + 1) * tile)
            normed, _ = normalize(x_ref[s, t * tile : (t + 1) * tile])
            value = (normed * gain_ref[...].astype(F32) + bias_ref[...].astype(F32)).astype(BF16)
            mlp_in[here] = value
            mlp_in_t[:, here] = value.T
            gt[here] = gt_ref[2 * t : 2 * t + 2, s].reshape(tile, width)
            acc[here] = jnp.zeros((tile, width), F32)
            gacc[here] = jnp.zeros((tile, width), F32)

    b1 = b1_ref[...].astype(F32)
    db1 = jnp.zeros((1, columns), F32)
    for i in range(tiles):
        here = slice(i * tile, (i + 1) * tile)
        value, slope = gelu_both(dot(mlp_in[here], w1_ref[...]) + b1)
        value = value.astype(BF16)
        act[here] = value
        g = (dot(gt[here], w2_ref[...], NT) * slope).astype(BF16)
        gpre[here] = g
        db1 = db1 + row_sum(g)
        acc[here] += dot(value, w2_ref[...])
        gacc[here] += dot(g, w1_ref[...], NT)
    db1_ref[...] = db1
    if packed:
        step = 192
        for i in range(width // step):
            store_packed(dw1_ref, "xy", dot(mlp_in_t[i * step : (i + 1) * step], gpre[...]), i * step, 0)
        result = dot(act[...], gt[...], TN)
        for k in range(columns // 96):
            where = owner_dims(k, "yx")[:3] + (0,)
            dw2_ref[where] = result[k * 96 : (k + 1) * 96].astype(BF16)
    else:
        dw1_ref[...] = dot(mlp_in_t[...], gpre[...])
        dw2_ref[...] = dot(act[...], gt[...], TN)

    @pl.when(j == pl.num_programs(0) - 1)
    def _():
        gain = gain_ref[...].astype(F32)
        sums = [jnp.zeros((1, width), F32) for _ in range(4)]
        for i in range(tiles):
            s, t = i // per_sample, i % per_sample
            here = slice(i * tile, (i + 1) * tile)
            x = x_ref[s, t * tile : (t + 1) * tile]
            normed, inverse = normalize(x)
            mixed = (x + acc[here] + b2_ref[...].astype(F32)).astype(BF16)
            mixed_ref[2 * t : 2 * t + 2, s] = mixed.reshape(2, piece, width)
            cot = gt[here].astype(F32)
            g = gacc[here]
            gmid = cot + normalize_back(g * gain, normed, inverse)
            gmid_ref[s, t * tile : (t + 1) * tile] = gmid
            low = gmid.astype(BF16)
            gone_ref[s, t * tile : (t + 1) * tile] = low
            sums = [a + row_sum(b) for a, b in zip(sums, (g * normed, g, cot, low))]
        for k in range(4):
            small_ref[k : k + 1] = sums[k]


def mlp(packed, x, gt, w1, b1, w2, b2, gain, bias):
    samples, rows, width = x.shape
    parts, _, piece, _ = gt.shape
    hidden = w1.shape[1]
    columns = 768 if hidden % 768 == 0 else hidden
    tokens = samples * rows
    if packed:
        dw1 = ((2, 2, 2, 4, 24 * hidden // 128, 128), BF16)
        dw1_spec = pl.BlockSpec((2, 2, 2, 4, 24 * columns // 128, 128), lambda j: (0, 0, 0, 0, j, 0))
        dw2 = ((2, 2, 2, 4, 96, width), BF16)
        dw2_spec = pl.BlockSpec((2, 2, 2, 1, 96, width), lambda j: (0, 0, 0, j, 0, 0))
    else:
        dw1 = ((width, hidden), F32)
        dw1_spec = pl.BlockSpec((width, columns), lambda j: (0, j))
        dw2 = ((hidden, width), F32)
        dw2_spec = pl.BlockSpec((columns, width), lambda j: (j, 0))
    shapes = [
        ((parts, samples, piece, width), BF16),
        (x.shape, F32),
        (x.shape, BF16),
        dw1,
        dw2,
        ((1, hidden), F32),
        ((4, width), F32),
    ]
    return pl.pallas_call(
        functools.partial(mlp_kernel, packed),
        grid=(hidden // columns,),
        in_specs=[
            whole(x.shape),
            whole(gt.shape),
            pl.BlockSpec((width, columns), lambda j: (0, j)),
            pl.BlockSpec((1, columns), lambda j: (0, j)),
            pl.BlockSpec((columns, width), lambda j: (j, 0)),
            whole((1, width)),
            whole((1, width)),
            whole((1, width)),
        ],
        out_specs=[
            whole(shapes[0][0]),
            whole(x.shape),
            whole(x.shape),
            dw1_spec,
            dw2_spec,
            pl.BlockSpec((1, columns), lambda j: (0, j)),
            whole((4, width)),
        ],
        out_shape=[jax.ShapeDtypeStruct(*s) for s in shapes],
        scratch_shapes=[
            pltpu.VMEM((tokens, width), BF16),
            pltpu.VMEM((width, tokens), BF16),
            pltpu.VMEM((tokens, width), BF16),
            pltpu.VMEM((tokens, columns), BF16),
            pltpu.VMEM((tokens, columns), BF16),
            pltpu.VMEM((tokens, width), F32),
            pltpu.VMEM((tokens, width), F32),
        ],
        compiler_params=pltpu.CompilerParams(vmem_limit_bytes=60 * MIB),
        cost_estimate=pl.CostEstimate(flops=30 * 10**9, bytes_accessed=30 * 10**6, transcendentals=0),
        name="mlp",
    )(x, gt, w1, b1, w2, b2, gain, bias)


def attend_back_kernel(gone_ref, low_ref, joined_ref, probs_ref, wproj_ref, gjoined_ref, gatt, delta):
    j = pl.program_id(1)
    _, rows, width = gone_ref.shape
    half = 64

    @pl.when(j == 0)
    def _():
        grad = dot(gone_ref[0], wproj_ref[...], NT).astype(BF16)
        gatt[...] = grad
        product = grad.astype(F32) * low_ref[0].astype(F32)
        high = product.astype(BF16)
        rest = (product - high.astype(F32)).astype(BF16)
        heads = lax.broadcasted_iota(jnp.int32, (16, width), 0)
        owner = lax.broadcasted_iota(jnp.int32, (16, width), 1) // half
        pick = (heads == owner).astype(F32).astype(BF16)
        delta[...] = dot(pick, high, NT) + dot(pick, rest, NT)

    at = pl.multiple_of(j * 128, 128)
    at_k = pl.multiple_of(width + j * 128, 128)
    at_v = pl.multiple_of(2 * width + j * 128, 128)
    q = joined_ref[0, :, pl.ds(at, 128)]
    k = joined_ref[0, :, pl.ds(at_k, 128)]
    v = joined_ref[0, :, pl.ds(at_v, 128)]
    g = gatt[:, pl.ds(at, 128)]
    k_t = k.T
    left = lax.broadcasted_iota(jnp.int32, (rows, 128), 1) < half
    g_q, g_k, g_v = [], [], []
    for h in range(2):
        g_h = jnp.where(left == (h == 0), g, jnp.zeros_like(g))
        probs = probs_ref[0, h]
        back = dot(v, g_h, NT) - delta[pl.ds(2 * j + h, 1), :]
        scores = (probs.astype(F32) * back).astype(BF16)
        g_v.append(dot(probs, g))
        g_k.append(dot(scores, q))
        g_q.append(dot(k_t[h * half : (h + 1) * half], scores))
    gjoined_ref[0, :, pl.ds(at, 128)] = (jnp.concatenate(g_q, 0).T * half**-0.5).astype(BF16)
    gjoined_ref[0, :, pl.ds(at_k, 128)] = jnp.where(left, g_k[0], g_k[1]).astype(BF16)
    gjoined_ref[0, :, pl.ds(at_v, 128)] = jnp.where(left, g_v[0], g_v[1]).astype(BF16)


def attend_back(gone, low, joined, probs, w_proj):
    samples, rows, width = gone.shape
    by_sample = lambda shape: pl.BlockSpec((1,) + shape, lambda s, j: (s, 0, 0))
    return pl.pallas_call(
        attend_back_kernel,
        grid=(samples, HEADS // 2),
        in_specs=[
            by_sample((rows, width)),
            by_sample((rows, width)),
            by_sample((rows, 3 * width)),
            pl.BlockSpec((1, 2, rows, rows), lambda s, j: (s, j, 0, 0)),
            whole(w_proj.shape),
        ],
        out_specs=by_sample((rows, 3 * width)),
        out_shape=jax.ShapeDtypeStruct((samples, rows, 3 * width), BF16),
        scratch_shapes=[pltpu.VMEM((rows, width), BF16), pltpu.VMEM((16, rows), F32)],
        compiler_params=pltpu.CompilerParams(vmem_limit_bytes=56 * MIB),
        cost_estimate=pl.CostEstimate(flops=20 * 10**9, bytes_accessed=30 * 10**6, transcendentals=0),
        name="attend_back",
    )(gone, low, joined, probs, w_proj)


def finish_kernel(
    packed, misc_cols, gjoined_ref, w_ref, stream_ref, gmid_ref, gone_ref, low_ref, ids_ref, gain_ref, bias_ref, small_ref, db1_ref,
    dwqkv_ref, misc_ref, pgrad_ref, normed, inverse, attn_in_t, gacc, sums,
):
    j = pl.program_id(0)
    samples, rows, width = stream_ref.shape
    tokens = samples * rows
    piece = pgrad_ref.shape[2]
    positions = misc_cols - width - 128
    tile = 2 * piece
    per_sample = rows // tile
    tiles = samples * per_sample
    step = 192

    def put(first_tile, lhs, rhs):
        if packed:
            for i in range(width // step):
                result = dot(lhs[i * step : (i + 1) * step], rhs)
                store_packed(misc_ref, "yx", result, i * step, first_tile)
        else:
            misc_ref[:, first_tile * 128 : first_tile * 128 + rhs.shape[1]] = dot(lhs, rhs)

    @pl.when(j == 0)
    def _():
        for i in range(tiles):
            s, t = i // per_sample, i % per_sample
            here = slice(i * tile, (i + 1) * tile)
            n, inv = normalize(stream_ref[s, t * tile : (t + 1) * tile])
            normed[here] = n
            inverse[here] = inv
            value = (n * gain_ref[...].astype(F32) + bias_ref[...].astype(F32)).astype(BF16)
            attn_in_t[:, here] = value.T
            gacc[here] = jnp.zeros((tile, width), F32)
        put(0, low_ref[...].reshape(tokens, width).T, gone_ref[...].reshape(tokens, width))

    g = gjoined_ref[...].reshape(tokens, width)
    for i in range(tiles):
        here = slice(i * tile, (i + 1) * tile)
        gacc[here] += dot(g[here], w_ref[...], NT)
    sums[pl.ds(j, 1)] = row_sum(g)
    if packed:
        for i in range(width // step):
            store_packed(dwqkv_ref, "xy", dot(attn_in_t[i * step : (i + 1) * step], g), i * step, 0)
    else:
        dwqkv_ref[...] = dot(attn_in_t[...], g)

    @pl.when(j == pl.num_programs(0) - 1)
    def _():
        gain = gain_ref[...].astype(F32)
        g_gain = jnp.zeros((1, width), F32)
        g_bias = jnp.zeros((1, width), F32)
        hots = []
        for i in range(tiles):
            s, t = i // per_sample, i % per_sample
            here = slice(i * tile, (i + 1) * tile)
            n = normed[here]
            grad = gacc[here]
            total = gmid_ref[s, t * tile : (t + 1) * tile] + normalize_back(grad * gain, n, inverse[here])
            low = total.astype(BF16)
            pgrad_ref[2 * t : 2 * t + 2, s] = low.reshape(2, piece, width)
            attn_in_t[:, here] = low.T
            g_gain = g_gain + row_sum(grad * n)
            g_bias = g_bias + row_sum(grad)
            ids = ids_ref[s, t * tile : (t + 1) * tile]
            hots.append((ids == lax.broadcasted_iota(jnp.int32, (tile, positions), 1)).astype(F32).astype(BF16))
        zero = jnp.zeros((1, width), F32)
        few = [g_gain, g_bias, sums[0:1], sums[2:3], small_ref[3:4], small_ref[0:1], small_ref[1:2], small_ref[2:3]]
        few += [db1_ref[...]] + [zero] * 4
        few = jnp.concatenate(few, 0)
        few_t = jnp.concatenate([few, jnp.zeros((112, width), F32)], 0).T
        hot = jnp.concatenate(hots, 0)
        if packed:
            for i in range(width // step):
                cut = slice(i * step, (i + 1) * step)
                result = jnp.concatenate([dot(attn_in_t[cut], hot), few_t[cut]], 1)
                store_packed(misc_ref, "yx", result, i * step, 6)
        else:
            misc_ref[:, width:] = jnp.concatenate([dot(attn_in_t[...], hot), few_t], 1)


def finish(packed, gjoined, w_qkv, stream, gmid, gone, low, ids, gain, bias, small, db1, parts, positions):
    samples, rows, width = stream.shape
    tokens = samples * rows
    piece = rows // parts
    misc_cols = width + positions + 128
    if packed:
        dwqkv = ((2, 2, 2, 4, 24 * 18, 128), BF16)
        dwqkv_spec = pl.BlockSpec((2, 2, 2, 4, 24 * 6, 128), lambda j: (0, 0, 0, 0, j, 0))
        misc = ((2, 2, 2, 4, 24 * misc_cols // 128, 128), BF16)
    else:
        dwqkv = ((width, 3 * width), F32)
        dwqkv_spec = pl.BlockSpec((width, width), lambda j: (0, j))
        misc = ((width, misc_cols), F32)
    pgrad = ((parts, samples, piece, width), BF16)
    return pl.pallas_call(
        functools.partial(finish_kernel, packed, misc_cols),
        grid=(3,),
        in_specs=[
            pl.BlockSpec((samples, rows, width), lambda j: (0, 0, j)),
            pl.BlockSpec((width, width), lambda j: (0, j)),
        ]
        + [whole(a.shape) for a in (stream, gmid, gone, low, ids, gain, bias, small, db1)],
        out_specs=[dwqkv_spec, whole(misc[0]), whole(pgrad[0])],
        out_shape=[jax.ShapeDtypeStruct(*s) for s in (dwqkv, misc, pgrad)],
        scratch_shapes=[
            pltpu.VMEM((tokens, width), F32),
            pltpu.VMEM((tokens, 1), F32),
            pltpu.VMEM((width, tokens), BF16),
            pltpu.VMEM((tokens, width), F32),
            pltpu.VMEM((8, width), F32),
        ],
        compiler_params=pltpu.CompilerParams(vmem_limit_bytes=60 * MIB),
        cost_estimate=pl.CostEstimate(flops=12 * 10**9, bytes_accessed=30 * 10**6, transcendentals=0),
        name="finish",
    )(gjoined, w_qkv, stream, gmid, gone, low, ids, gain, bias, small, db1)


def swap_bit(x, bit, count):
    return lax.ppermute(x, AXES, [(i, i ^ bit) for i in range(count)])


def reduce_packed(grad, order, count):
    here = lax.axis_index(AXES)
    x = lax.psum_scatter(grad, "blk", scatter_dimension=0, tiled=False, axis_index_groups=[[0, 1], [2, 3]])
    for name in order:
        bit = {"x": 4, "y": 2}[name]
        mine = (here // bit) % 2
        keep = lax.dynamic_index_in_dim(x, mine, 0, keepdims=False)
        send = lax.dynamic_index_in_dim(x, 1 - mine, 0, keepdims=False)
        x = keep + swap_bit(send, bit, count)
    pieces = lax.all_to_all(x, "wide", 0, 0, axis_index_groups=[[0, 2, 4, 6], [1, 3, 5, 7]], tiled=True)
    return jnp.sum(pieces.astype(F32), axis=0)


def unpack(x):
    tiles = x.shape[0] // 24
    return jnp.transpose(x.reshape(tiles, 24, 128), (1, 0, 2)).reshape(24, tiles * 128)


def shards(
    patches, pos_ids, lengths, pos_table, ln1_gain, ln1_bias, w_qkv, q_bias, v_bias, w_proj, proj_bias,
    ln2_gain, ln2_bias, w_fc1, fc1_bias, w_fc2, fc2_bias, cotangent, *, wide, parts,
):
    samples_here, piece, width = patches.shape
    samples = samples_here // parts
    rows = parts * piece
    count = wide * parts
    packed = wide == 8 and parts == 4
    row = lambda a: a.reshape(1, -1)
    swap = lambda a: lax.all_to_all(a, "blk", 0, 0, tiled=True)

    cut = patches.reshape(parts, samples, piece, width)
    xs = [swap(cut[:, s : s + 1]) for s in range(samples)]
    ids = swap(pos_ids.reshape(parts, samples, piece))
    ids = jnp.transpose(ids, (1, 0, 2)).reshape(samples, rows, 1)
    me = lax.axis_index("blk")
    own_lengths = lax.dynamic_slice_in_dim(lengths, me * samples, samples)
    gt = swap(cotangent.reshape(parts, samples, piece, width))
    b_qkv = row(jnp.concatenate([q_bias, jnp.zeros_like(q_bias), v_bias]))

    saved = None
    for s in range(samples):
        saved = attend(
            s, samples, own_lengths[s : s + 1], xs[s], ids, pos_table, row(ln1_gain), row(ln1_bias),
            w_qkv, b_qkv, w_proj, row(proj_bias), saved,
        )
    stream, joined, probs, low, mid = saved
    mixed, gmid, gone, dw1, dw2, db1, small = mlp(
        packed, mid, gt, w_fc1, row(fc1_bias), w_fc2, row(fc2_bias), row(ln2_gain), row(ln2_bias)
    )
    mixed = swap(mixed).reshape(patches.shape)
    gjoined = attend_back(gone, low, joined, probs, w_proj)
    dwqkv, misc, pgrad = finish(
        packed, gjoined, w_qkv, stream, gmid, gone, low, ids, row(ln1_gain), row(ln1_bias), small,
        jnp.transpose(db1.reshape(width, -1)), parts, pos_table.shape[1],
    )
    pgrad = swap(pgrad).reshape(patches.shape)
    if packed:
        dw1 = unpack(reduce_packed(dw1, "xy", count))
        dw2 = reduce_packed(dw2, "yx", count)
        dwqkv = unpack(reduce_packed(dwqkv, "xy", count))
        misc = unpack(reduce_packed(misc, "yx", count))
    else:
        share = lambda a: lax.psum_scatter(a.astype(BF16), AXES, scatter_dimension=0, tiled=True).astype(F32)
        dw1, dw2, dwqkv, misc = share(dw1), share(dw2), share(dwqkv), share(misc)
    dwproj, table, few = misc[:, :width], misc[:, width:-128], misc[:, -128:]
    (g_gain1, g_bias1, g_q, g_v, g_proj, g_gain2, g_bias2, g_fc2) = [few[:, k] for k in range(8)]
    g_fc1 = few[:, 8:12].reshape(-1)
    return (
        mixed, pgrad, table, g_gain1, g_bias1, dwqkv, g_q, g_v, dwproj, g_proj, g_gain2, g_bias2,
        dw1, g_fc1, dw2, g_fc2,
    )


def solution(mesh):
    wide, parts = mesh.shape["wide"], mesh.shape["blk"]
    tokens = P("wide", "blk", None)
    in_specs = (tokens, P("wide", "blk"), P("wide")) + (P(),) * 14 + (tokens,)
    vector, matrix = P(AXES), P(AXES, None)
    out_specs = (
        tokens, tokens, matrix, vector, vector, matrix, vector, vector, matrix, vector, vector, vector,
        matrix, vector, matrix, vector,
    )
    return jax.shard_map(
        functools.partial(shards, wide=wide, parts=parts),
        mesh=mesh, in_specs=in_specs, out_specs=out_specs, check_vma=False,
    )
```

time: 1030 us -> 352 us (0.34)
  waiting for transfers between devices: 623 us -> 93.9 us
  matrix products: 229 us -> 0 us
  Pallas kernels: 0 us -> 128 us
  starting transfers between devices: 1.2 us -> 47.7 us
  local copies, waits for them, and re-layouts: 72.9 us -> 33.5 us
  blocking collectives: 41.4 us -> 14.9 us
  other arithmetic: 39.6 us -> 18.3 us
    reduce_scatter x5 -> x4, waiting for transfers between devices: 471 us -> 35.1 us  [reduce_packed(): lax.psum_scatter(grad, 'blk', scatter_dimension=0, tiled=False, axis_inde...]
    dot_general x20 -> x0, matrix products: 229 us -> none  [the longest x4 54.4 us: product(): return jnp.dot(remaining_part, right, preferred_element_type=jnp.float32)]
    pallas_call x0 -> x5, Pallas kernels: none -> 128 us  [the longest x1 42.2 us: mlp(): pl.pallas_call(functools.partial(mlp_kernel, packed), grid=(hidden // col...]
    unnamed x9 -> x4, waiting for transfers between devices: 104 us -> 1.92 us
    all_gather x2 -> x0, waiting for transfers between devices: 47.4 us -> none  [the longest x1 38.6 us: shards(): lax.all_gather(key_rows, 'blk', axis=1, tiled=True)]
    unnamed x1 -> x0, blocking collectives: 41.4 us -> none
    ppermute x0 -> x8, waiting for transfers between devices: none -> 38.4 us  [swap_bit(): return lax.ppermute(x, AXES, [(i, i ^ bit) for i in range(count)])]
    all_to_all x0 -> x9, starting transfers between devices: none -> 37.1 us  [the longest x4 18.6 us: reduce_packed(): lax.all_to_all(x, 'wide', 0, 0, axis_index_groups=[[0, 2, 4, 6], [1, 3, 5...]
  transfers between devices with their start and end apart: 8 -> 21, of which waited for: 8 -> 12; matrix products, arithmetic and copies ran while one was open for 14% -> 12% of each run, Pallas kernels for 0% -> 11%
where the time goes in v1:
time: 352 us; the launch traced here: 351 us
  Pallas kernels  128 us (36%)
  waiting for transfers between devices  93.9 us (27%)
  starting transfers between devices  47.7 us (14%)
  local copies, waits for them, and re-layouts  33.5 us (10%)
  other arithmetic  18.3 us (5%)
  blocking collectives  14.9 us (4%)
  between operations  14.1 us (4%)
    pallas_call x1, Pallas kernels, mlp(): pl.pallas_call(functools.partial(mlp_kernel, packed), grid=(hidden // col...  42.2 us
    pallas_call x2, Pallas kernels, attend(): pl.pallas_call(attend_kernel, grid=(pairs,), in_specs=in_specs, out_specs...  40 us
    ppermute x8, waiting for transfers between devices, swap_bit(): return lax.ppermute(x, AXES, [(i, i ^ bit) for i in range(count)])  38.4 us
    reduce_scatter x4, waiting for transfers between devices, reduce_packed(): lax.psum_scatter(grad, 'blk', scatter_dimension=0, tiled=False, axis_inde...  35.1 us
    pallas_call x1, Pallas kernels, attend_back(): pl.pallas_call(attend_back_kernel, grid=(samples, HEADS // 2), in_specs=[...  25.3 us
    pallas_call x1, Pallas kernels, finish(): pl.pallas_call(functools.partial(finish_kernel, packed, misc_cols), grid=...  20.6 us
    all_to_all x4, starting transfers between devices, reduce_packed(): lax.all_to_all(x, 'wide', 0, 0, axis_index_groups=[[0, 2, 4, 6], [1, 3, 5...  18.6 us
    all_to_all x5, starting transfers between devices, shards(): swap = lambda a: lax.all_to_all(a, 'blk', 0, 0, tiled=True)  18.4 us
  transfers between devices with their start and end apart: 21, of which 12 were waited for; matrix products, arithmetic and copies ran while one was open for 12% of the time, Pallas kernels for 11%

profile of v1, /device:TPU:0, one launch (start us, length us, event | category | flops | bytes accessed | tf_op | source)
XLA Modules:
  0.0 350.6 jit_solution(3062805738102924618)
XLA Ops:
  7.2 4.2 %all-to-all-start.1 = ((s32[4,2,128]{2,1,0:T(2,128)}), s32[4,2,128]{2,1,0:T(2,128)S(1)}, u32[]{:S(2)}, u32[]{:S(2)}) async-start(s32[4,2,128]{2,1,0:T(2,128)} %bitcast.76), calls=%async_computation.1 | async-start | bytes 8192 | tf_op jit(solution)/shard_map/all_to_all | solution.py:508
  15.3 14.9 %all_to_all.50.x_ref = bf16[4,1,128,768]{3,2,1,0:T(8,128)(2,1)} all-to-all(bf16[4,1,128,768]{3,2,1,0:T(8,128)(2,1)S(1)} %get-tuple-element.65), channel_id=1, replica_groups=mesh['wide'=8,'blk'=4] {'blk'}, dimensions={0} | all-to-all | bytes 1572864 | tf_op jit(solution)/shard_map/all_to_all | solution.py:508
  40.2 5.1 %all-to-all-done.2.x_ref = bf16[4,1,128,768]{3,2,1,0:T(8,128)(2,1)S(1)} async-done(((bf16[4,1,128,768]{3,2,1,0:T(8,128)(2,1)}), bf16[4,1,128,768]{3,2,1,0:T(8,128)(2,1)S(1)}, u32[]{:S(2)}, u32[]{:S(2)}) %all-to-all-start.2) | async-done | bytes 786464 | tf_op jit(solution)/shard_map/all_to_all | solution.py:508
  46.2 3.6 %all-to-all-start.3 = ((bf16[4,2,128,768]{3,2,1,0:T(8,128)(2,1)}), bf16[4,2,128,768]{3,2,1,0:T(8,128)(2,1)S(1)}, u32[]{:S(2)}, u32[]{:S(2)}) async-start(bf16[4,2,128,768]{3,2,1,0:T(8,128)(2,1)} %bitcast.4), calls=%async_computation.3 | async-start | bytes 3145728 | tf_op jit(solution)/shard_map/all_to_all | solution.py:508
  49.8 19.9 %attend_0.1 = (f32[2,512,768]{2,1,0:T(8,128)}, bf16[2,512,2304]{2,1,0:T(8,128)(2,1)}, bf16[2,12,512,512]{3,2,1,0:T(8,128)(2,1)}, bf16[2,512,768]{2,1,0:T(8,128)(2,1)}, f32[2,512,768]{2,1,0:T(8,128)}) custom-call(s32[1]{0:T(128)} %get-tuple-element.66.length_ref, bf16[4,1,128,768]{3,2,1,0:T(8,128)(2,1)} %copy-done.9, s32[2,512,1]{2,1,0:T(8,128)} %copy.56.ids_ref, ...), custom_call_target="tpu_custom_call" | custom-call | flops 12000000000 | bytes 30000000 | tf_op jit(solution)/shard_map/attend_0/pallas_call | solution.py:137
  69.8 20.1 %attend_1.1 = (f32[2,512,768]{2,1,0:T(8,128)}, bf16[2,512,2304]{2,1,0:T(8,128)(2,1)}, bf16[2,12,512,512]{3,2,1,0:T(8,128)(2,1)}, bf16[2,512,768]{2,1,0:T(8,128)(2,1)}, f32[2,512,768]{2,1,0:T(8,128)}) custom-call(s32[1]{0:T(128)} %get-tuple-element.67.length_ref, ...), custom_call_target="tpu_custom_call", output_to_operand_aliasing={{0}: (10, {}), {1}: (11, {}), {2}: (12, {}), {3}: (13, {}),... | custom-call | flops 12000000000 | bytes 30000000 | tf_op jit(solution)/shard_map/attend_1/pallas_call | solution.py:137
  91.0 42.2 %mlp.1 = (bf16[4,2,128,768]{3,2,1,0:T(8,128)(2,1)}, f32[2,512,768]{2,1,0:T(8,128)}, bf16[2,512,768]{2,1,0:T(8,128)(2,1)}, bf16[2,2,2,4,576,128]{5,4,3,2,1,0:T(8,...) custom-call(f32[2,512,768]{2,1,0:T(8,128)} %get-tuple-element.41.x_ref, ...), custom_call_target="tpu_custom_call" | custom-call | flops 30000001024 | bytes 30000000 | tf_op jit(solution)/shard_map/mlp/pallas_call | solution.py:259
  136.2 25.3 %attend_back.1.gjoined_ref = bf16[2,512,2304]{2,1,0:T(8,128)(2,1)} custom-call(bf16[2,512,768]{2,1,0:T(8,128)(2,1)} %get-tuple-element.43.gone_ref, bf16[2,512,768]{2,1,0:T(8,128)(2,1)} %get-tuple-element.44.low_ref, bf16[2,512,2304]{2,1,0:T(8,128)(2,1)} %get-tuple-element.45.joined_ref, bf16[2,12,512,512]{3,2,1,0:T(8,128)(2,1)} %get-tuple-element.46.probs_ref, ...), custom_call_target="tpu_custom_call" | custom-call | flops 20000000000 | bytes 30000000 | tf_op jit(solution)/shard_map/attend_back/pallas_call | solution.py:340
  161.6 20.6 %finish.1 = (bf16[2,2,2,4,432,128]{5,4,3,2,1,0:T(8,128)(2,1)}, bf16[2,2,2,4,288,128]{5,4,3,2,1,0:T(8,128)(2,1)}, bf16[4,2,128,768]{3,2,1,0:T(8,128)(2,1)}) custom-call(bf16[2,512,2304]{2,1,0:T(8,128)(2,1)} %attend_back.1.gjoined_ref, bf16[768,2304]{1,0:T(8,128)(2,1)} %w_ref.1, f32[2,512,768]{2,1,0:T(8,128)} %get-tuple-element.47.stream_ref, ...), custom_call_target="tpu_custom_call" | custom-call | flops 12000000000 | bytes 30000000 | tf_op jit(solution)/shard_map/finish/pallas_call | solution.py:453
  184.3 3.6 %all-to-all-start.4 = ((bf16[4,2,128,768]{3,2,1,0:T(8,128)(2,1)}), bf16[4,2,128,768]{3,2,1,0:T(8,128)(2,1)S(1)}, u32[]{:S(2)}, u32[]{:S(2)}) async-start(bf16[4,2,128,768]{3,2,1,0:T(8,128)(2,1)} %get-tuple-element.42), calls=%async_computation.4 | async-start | bytes 3145728 | tf_op jit(solution)/shard_map/all_to_all | solution.py:508
  187.9 6.5 %reduce-scatter.5.cloned.1.call-done = bf16[1,2,2,4,288,128]{5,4,3,2,1,0:T(8,128)(2,1)} async-done(((bf16[2,2,2,4,288,128]{5,4,3,2,1,0:T(8,128)(2,1)}), bf16[1,2,2,4,288,128]{5,4,3,2,1,0:T(8,128)(2,1)}) %reduce-scatter.5.cloned.1.call-update) | async-done | bytes 1179664 | tf_op jit(solution)/shard_map/reduce_scatter | solution.py:482
  198.0 11.2 %reduce-scatter.7.cloned.1.call-done = bf16[1,2,2,4,432,128]{5,4,3,2,1,0:T(8,128)(2,1)} async-done(((bf16[2,2,2,4,432,128]{5,4,3,2,1,0:T(8,128)(2,1)}), bf16[1,2,2,4,432,128]{5,4,3,2,1,0:T(8,128)(2,1)}) %reduce-scatter.7.cloned.1.call-update) | async-done | bytes 1769488 | tf_op jit(solution)/shard_map/reduce_scatter | solution.py:482
  213.1 3.6 %all-to-all-start.5 = ((bf16[4,2,128,768]{3,2,1,0:T(8,128)(2,1)}), bf16[4,2,128,768]{3,2,1,0:T(8,128)(2,1)S(1)}, u32[]{:S(2)}, u32[]{:S(2)}) async-start(bf16[4,2,128,768]{3,2,1,0:T(8,128)(2,1)} %get-tuple-element.51), calls=%async_computation.5 | async-start | bytes 3145728 | tf_op jit(solution)/shard_map/all_to_all | solution.py:508
  216.7 8.6 %reduce-scatter.9.cloned.1.call-done = bf16[1,2,2,4,576,128]{5,4,3,2,1,0:T(8,128)(2,1)} async-done(((bf16[2,2,2,4,576,128]{5,4,3,2,1,0:T(8,128)(2,1)}), bf16[1,2,2,4,576,128]{5,4,3,2,1,0:T(8,128)(2,1)}) %reduce-scatter.9.cloned.1.call-update) | async-done | bytes 2359312 | tf_op jit(solution)/shard_map/reduce_scatter | solution.py:482
  232.6 8.8 %reduce-scatter.11.cloned.1.call-done = bf16[1,2,2,4,96,768]{5,4,3,2,1,0:T(8,128)(2,1)} async-done(((bf16[2,2,2,4,96,768]{5,4,3,2,1,0:T(8,128)(2,1)}), bf16[1,2,2,4,96,768]{5,4,3,2,1,0:T(8,128)(2,1)}) %reduce-scatter.11.cloned.1.call-update) | async-done | bytes 2359312 | tf_op jit(solution)/shard_map/reduce_scatter | solution.py:482
  248.1 16.9 %collective-permute-done.1 = bf16[4,288,128]{2,1,0:T(8,128)(2,1)S(1)} collective-permute-done((bf16[4,288,128]{2,1,0:T(8,128)(2,1)}, bf16[4,288,128]{2,1,0:T(8,128)(2,1)S(1)}, u32[]{:S(2)}, u32[]{:S(2)}) %collective-permute-start.1) | collective-permute-done | bytes 294944 | tf_op jit(solution)/shard_map/ppermute | solution.py:477
  265.8 4.9 %all-to-all-start.6 = ((bf16[4,288,128]{2,1,0:T(8,128)(2,1)}), bf16[4,288,128]{2,1,0:T(8,128)(2,1)S(1)}, u32[]{:S(2)}, u32[]{:S(2)}) async-start(bf16[4,288,128]{2,1,0:T(8,128)(2,1)} %bitcast_add_fusion.7), calls=%async_computation.7 | async-start | bytes 589824 | tf_op jit(solution)/shard_map/all_to_all | solution.py:489
  275.9 6.6 %collective-permute-done.3 = bf16[4,432,128]{2,1,0:T(8,128)(2,1)} collective-permute-done((bf16[4,432,128]{2,1,0:T(8,128)(2,1)}, bf16[4,432,128]{2,1,0:T(8,128)(2,1)}, u32[]{:S(2)}, u32[]{:S(2)}) %collective-permute-start.3) | collective-permute-done | bytes 442400 | tf_op jit(solution)/shard_map/ppermute | solution.py:477
  284.4 4.8 %all-to-all-start.7 = ((bf16[4,432,128]{2,1,0:T(8,128)(2,1)}), bf16[4,432,128]{2,1,0:T(8,128)(2,1)}, u32[]{:S(2)}, u32[]{:S(2)}) async-start(bf16[4,432,128]{2,1,0:T(8,128)(2,1)} %bitcast_add_fusion.6), calls=%async_computation.9 | async-start | bytes 884736 | tf_op jit(solution)/shard_map/all_to_all | solution.py:489
  296.5 4.6 %all-to-all-done.7 = bf16[4,432,128]{2,1,0:T(8,128)(2,1)} async-done(((bf16[4,432,128]{2,1,0:T(8,128)(2,1)}), bf16[4,432,128]{2,1,0:T(8,128)(2,1)}, u32[]{:S(2)}, u32[]{:S(2)}) %all-to-all-start.7) | async-done | bytes 442400 | tf_op jit(solution)/shard_map/all_to_all | solution.py:489
  301.1 4.2 %all-to-all-start.8 = ((bf16[4,576,128]{2,1,0:T(8,128)(2,1)}), bf16[4,576,128]{2,1,0:T(8,128)(2,1)}, u32[]{:S(2)}, u32[]{:S(2)}) async-start(bf16[4,576,128]{2,1,0:T(8,128)(2,1)} %bitcast_add_fusion.4), calls=%async_computation.11 | async-start | bytes 1179648 | tf_op jit(solution)/shard_map/all_to_all | solution.py:489
  308.1 12.4 %collective-permute-done.7 = bf16[4,96,768]{2,1,0:T(8,128)(2,1)S(1)} collective-permute-done((bf16[4,96,768]{2,1,0:T(8,128)(2,1)S(1)}, bf16[4,96,768]{2,1,0:T(8,128)(2,1)S(1)}, u32[]{:S(2)}, u32[]{:S(2)}) %collective-permute-start.7) | collective-permute-done | bytes 589856 | tf_op jit(solution)/shard_map/ppermute | solution.py:477
  321.3 4.8 %all-to-all-start.9 = ((bf16[4,96,768]{2,1,0:T(8,128)(2,1)}), bf16[4,96,768]{2,1,0:T(8,128)(2,1)}, u32[]{:S(2)}, u32[]{:S(2)}) async-start(bf16[4,96,768]{2,1,0:T(8,128)(2,1)} %bitcast_add_fusion.3), calls=%async_computation.13 | async-start | bytes 1179648 | tf_op jit(solution)/shard_map/all_to_all | solution.py:489
  332.6 7.3 %all-to-all-done.9 = bf16[4,96,768]{2,1,0:T(8,128)(2,1)} async-done(((bf16[4,96,768]{2,1,0:T(8,128)(2,1)}), bf16[4,96,768]{2,1,0:T(8,128)(2,1)}, u32[]{:S(2)}, u32[]{:S(2)}) %all-to-all-start.9) | async-done | bytes 589856 | tf_op jit(solution)/shard_map/all_to_all | solution.py:489
  (116 shorter events, 71.9 us)
Async XLA Ops:
  7.2 8.0 %all-to-all-start.1 = ((s32[4,2,128]{2,1,0:T(2,128)}), s32[4,2,128]{2,1,0:T(2,128)S(1)}, u32[]{:S(2)}, u32[]{:S(2)}) async-start(s32[4,2,128]{2,1,0:T(2,128)} %bitcast.76), calls=%async_computation.1 | async-start | bytes 8192 | tf_op jit(solution)/shard_map/all_to_all | solution.py:508
  15.3 22.1 %copy-start.15 = (bf16[768]{0:T(1024)(128)(2,1)S(1)}, bf16[768]{0:T(1024)(128)(2,1)}, u32[]{:S(2)}) copy-start(bf16[768]{0:T(1024)(128)(2,1)} %param.29) | copy-start | bytes 4612
  15.3 22.6 %copy-start.16 = (bf16[768]{0:T(1024)(128)(2,1)S(1)}, bf16[768]{0:T(1024)(128)(2,1)}, u32[]{:S(2)}) copy-start(bf16[768]{0:T(1024)(128)(2,1)} %param.30) | copy-start | bytes 4612
  15.3 23.2 %copy-start.19 = (s32[8]{0:T(128)S(1)}, s32[8]{0:T(128)}, u32[]{:S(2)}) copy-start(s32[8]{0:T(128)} %param.20) | copy-start | bytes 100
  30.2 15.1 %all-to-all-start.2 = ((bf16[4,1,128,768]{3,2,1,0:T(8,128)(2,1)}), bf16[4,1,128,768]{3,2,1,0:T(8,128)(2,1)S(1)}, u32[]{:S(2)}, u32[]{:S(2)}) async-start(bf16[4,1,128,768]{3,2,1,0:T(8,128)(2,1)} %get-tuple-element.64), calls=%async_computation.2 | async-start | bytes 1572864 | tf_op jit(solution)/shard_map/all_to_all | solution.py:508
  46.2 43.6 %all-to-all-start.3 = ((bf16[4,2,128,768]{3,2,1,0:T(8,128)(2,1)}), bf16[4,2,128,768]{3,2,1,0:T(8,128)(2,1)S(1)}, u32[]{:S(2)}, u32[]{:S(2)}) async-start(bf16[4,2,128,768]{3,2,1,0:T(8,128)(2,1)} %bitcast.4), calls=%async_computation.3 | async-start | bytes 3145728 | tf_op jit(solution)/shard_map/all_to_all | solution.py:508
  49.8 144.5 %reduce-scatter.5.cloned.1.call-start = ((), (), s32[]{:S(2)}) async-start(), calls=%async_computation.14 | async-start | bytes 3538944 | tf_op jit(solution)/shard_map/reduce_scatter | solution.py:482
  182.2 27.0 %reduce-scatter.7.cloned.1.call-start = ((), (), s32[]{:S(2)}) async-start(), calls=%async_computation.15 | async-start | bytes 5308416 | tf_op jit(solution)/shard_map/reduce_scatter | solution.py:482
  182.9 42.4 %reduce-scatter.9.cloned.1.call-start = ((), (), s32[]{:S(2)}) async-start(), calls=%async_computation.16 | async-start | bytes 7077888 | tf_op jit(solution)/shard_map/reduce_scatter | solution.py:482
  183.7 57.7 %reduce-scatter.11.cloned.1.call-start = ((), (), s32[]{:S(2)}) async-start(), calls=%async_computation.17 | async-start | bytes 7077888 | tf_op jit(solution)/shard_map/reduce_scatter | solution.py:482
  184.3 28.9 %all-to-all-start.4 = ((bf16[4,2,128,768]{3,2,1,0:T(8,128)(2,1)}), bf16[4,2,128,768]{3,2,1,0:T(8,128)(2,1)S(1)}, u32[]{:S(2)}, u32[]{:S(2)}) async-start(bf16[4,2,128,768]{3,2,1,0:T(8,128)(2,1)} %get-tuple-element.42), calls=%async_computation.4 | async-start | bytes 3145728 | tf_op jit(solution)/shard_map/all_to_all | solution.py:508
  196.3 33.2 %collective-permute-start = (bf16[2,4,288,128]{3,2,1,0:T(8,128)(2,1)}, bf16[2,4,288,128]{3,2,1,0:T(8,128)(2,1)}, u32[]{:S(2)}, u32[]{:S(2)}) collective-permute-start(bf16[2,4,288,128]{3,2,1,0:T(8,128)(2,1)} %dynamic-slice_bitcast_fusion.5), channel_id=1, source_target_pairs={{0,2},{1,3},{2,0},{3,1},{4,6},{5,7},{6,4},{7,5},{8,10},{9,11},{10,... | collective-permute-start | bytes 1769480 | tf_op jit(solution)/shard_map/ppermute | solution.py:477
  211.4 34.3 %collective-permute-start.2 = (bf16[2,4,432,128]{3,2,1,0:T(8,128)(2,1)}, bf16[2,4,432,128]{3,2,1,0:T(8,128)(2,1)}, u32[]{:S(2)}, u32[]{:S(2)}) collective-permute-start(bf16[2,4,432,128]{3,2,1,0:T(8,128)(2,1)} %dynamic-slice_bitcast_fusion.2), channel_id=1, source_target_pairs={{0,4},{1,5},{2,6},{3,7},{4,0},{5,1},{6,2},{7,3},{8,12},{9,13},{10,... | collective-permute-start | bytes 2654216 | tf_op jit(solution)/shard_map/ppermute | solution.py:477
  213.1 52.7 %all-to-all-start.5 = ((bf16[4,2,128,768]{3,2,1,0:T(8,128)(2,1)}), bf16[4,2,128,768]{3,2,1,0:T(8,128)(2,1)S(1)}, u32[]{:S(2)}, u32[]{:S(2)}) async-start(bf16[4,2,128,768]{3,2,1,0:T(8,128)(2,1)} %get-tuple-element.51), calls=%async_computation.5 | async-start | bytes 3145728 | tf_op jit(solution)/shard_map/all_to_all | solution.py:508
  227.7 43.0 %collective-permute-start.4 = (bf16[2,4,576,128]{3,2,1,0:T(8,128)(2,1)}, bf16[2,4,576,128]{3,2,1,0:T(8,128)(2,1)}, u32[]{:S(2)}, u32[]{:S(2)}) collective-permute-start(bf16[2,4,576,128]{3,2,1,0:T(8,128)(2,1)} %dynamic-slice_bitcast_fusion.1), channel_id=1, source_target_pairs={{0,4},{1,5},{2,6},{3,7},{4,0},{5,1},{6,2},{7,3},{8,12},{9,13},{10,... | collective-permute-start | bytes 3538952 | tf_op jit(solution)/shard_map/ppermute | solution.py:477
  232.3 32.7 %collective-permute-start.1 = (bf16[4,288,128]{2,1,0:T(8,128)(2,1)}, bf16[4,288,128]{2,1,0:T(8,128)(2,1)S(1)}, u32[]{:S(2)}, u32[]{:S(2)}) collective-permute-start(bf16[4,288,128]{2,1,0:T(8,128)(2,1)} %dynamic-slice_bitcast_fusion.7), channel_id=1, source_target_pairs={{0,4},{1,5},{2,6},{3,7},{4,0},{5,1},{6,2},{7,3},{8,12},{9,13},{10,... | collective-permute-start | bytes 884744 | tf_op jit(solution)/shard_map/ppermute | solution.py:477
  243.9 45.3 %collective-permute-start.6 = (bf16[2,4,96,768]{3,2,1,0:T(8,128)(2,1)}, bf16[2,4,96,768]{3,2,1,0:T(8,128)(2,1)}, u32[]{:S(2)}, u32[]{:S(2)}) collective-permute-start(bf16[2,4,96,768]{3,2,1,0:T(8,128)(2,1)} %dynamic-slice_bitcast_fusion), channel_id=1, source_target_pairs={{0,2},{1,3},{2,0},{3,1},{4,6},{5,7},{6,4},{7,5},{8,10},{9,11},{10,... | collective-permute-start | bytes 3538952 | tf_op jit(solution)/shard_map/ppermute | solution.py:477
  247.8 34.7 %collective-permute-start.3 = (bf16[4,432,128]{2,1,0:T(8,128)(2,1)}, bf16[4,432,128]{2,1,0:T(8,128)(2,1)}, u32[]{:S(2)}, u32[]{:S(2)}) collective-permute-start(bf16[4,432,128]{2,1,0:T(8,128)(2,1)} %dynamic-slice_bitcast_fusion.6), channel_id=1, source_target_pairs={{0,2},{1,3},{2,0},{3,1},{4,6},{5,7},{6,4},{7,5},{8,10},{9,11},{10,... | collective-permute-start | bytes 1327112 | tf_op jit(solution)/shard_map/ppermute | solution.py:477
  265.8 18.5 %all-to-all-start.6 = ((bf16[4,288,128]{2,1,0:T(8,128)(2,1)}), bf16[4,288,128]{2,1,0:T(8,128)(2,1)S(1)}, u32[]{:S(2)}, u32[]{:S(2)}) async-start(bf16[4,288,128]{2,1,0:T(8,128)(2,1)} %bitcast_add_fusion.7), calls=%async_computation.7 | async-start | bytes 589824 | tf_op jit(solution)/shard_map/all_to_all | solution.py:489
  274.4 20.1 %collective-permute-start.5 = (bf16[4,576,128]{2,1,0:T(8,128)(2,1)}, bf16[4,576,128]{2,1,0:T(8,128)(2,1)}, u32[]{:S(2)}, u32[]{:S(2)}) collective-permute-start(bf16[4,576,128]{2,1,0:T(8,128)(2,1)} %dynamic-slice_bitcast_fusion.4), channel_id=1, source_target_pairs={{0,2},{1,3},{2,0},{3,1},{4,6},{5,7},{6,4},{7,5},{8,10},{9,11},{10,... | collective-permute-start | bytes 1769480 | tf_op jit(solution)/shard_map/ppermute | solution.py:477
  284.4 16.8 %all-to-all-start.7 = ((bf16[4,432,128]{2,1,0:T(8,128)(2,1)}), bf16[4,432,128]{2,1,0:T(8,128)(2,1)}, u32[]{:S(2)}, u32[]{:S(2)}) async-start(bf16[4,432,128]{2,1,0:T(8,128)(2,1)} %bitcast_add_fusion.6), calls=%async_computation.9 | async-start | bytes 884736 | tf_op jit(solution)/shard_map/all_to_all | solution.py:489
  301.1 20.2 %all-to-all-start.8 = ((bf16[4,576,128]{2,1,0:T(8,128)(2,1)}), bf16[4,576,128]{2,1,0:T(8,128)(2,1)}, u32[]{:S(2)}, u32[]{:S(2)}) async-start(bf16[4,576,128]{2,1,0:T(8,128)(2,1)} %bitcast_add_fusion.4), calls=%async_computation.11 | async-start | bytes 1179648 | tf_op jit(solution)/shard_map/all_to_all | solution.py:489
  306.5 13.9 %collective-permute-start.7 = (bf16[4,96,768]{2,1,0:T(8,128)(2,1)S(1)}, bf16[4,96,768]{2,1,0:T(8,128)(2,1)S(1)}, u32[]{:S(2)}, u32[]{:S(2)}) collective-permute-start(bf16[4,96,768]{2,1,0:T(8,128)(2,1)S(1)} %dynamic-slice_bitcast_fusion.3), channel_id=1, source_target_pairs={{0,4},{1,5},{2,6},{3,7},{4,0},{5,1},{6,2},{7,3},{8,12},{9,13},{10,... | collective-permute-start | bytes 1769480 | tf_op jit(solution)/shard_map/ppermute | solution.py:477
  321.3 18.6 %all-to-all-start.9 = ((bf16[4,96,768]{2,1,0:T(8,128)(2,1)}), bf16[4,96,768]{2,1,0:T(8,128)(2,1)}, u32[]{:S(2)}, u32[]{:S(2)}) async-start(bf16[4,96,768]{2,1,0:T(8,128)(2,1)} %bitcast_add_fusion.3), calls=%async_computation.13 | async-start | bytes 1179648 | tf_op jit(solution)/shard_map/all_to_all | solution.py:489
  (17 other events, 219.3 us)
Sparse Core Ops, SparseCore 0:
  182.3 11.9 reduce-scatter.4
  196.7 12.5 reduce-scatter.6
  211.5 13.7 reduce-scatter.8
  227.6 13.7 reduce-scatter.10
